TPU v7x, 128 devices: a whole 4x4x4 slice. The times are simulated.
128 devices in a mesh: lat: 16 (over z_lo, x, core), lon: 8 (over z_hi, y).
Axes of the slice: x: 4, y: 4, z: 4 (z_hi: 2, z_lo: 2; z = z_hi * 2 + z_lo), core: 2. Of those that a mesh axis runs over, the one named last changes fastest.
Arguments:
- tokens: bfloat16 [8, 96, 192, 192], P(None, 'lat', 'lon'), may hold values from -6 to 6
- lat_valid: int32 [96], P('lat'), may hold values from 0 to 1, as said below
- gain_attn: bfloat16 [192], replicated, may hold values from 0.099609375 to 1.8984375
- w_qkv: bfloat16 [192, 576], replicated, may hold values from -0.4375 to 0.4375
- w_proj: bfloat16 [192, 192], replicated, may hold values from -0.4375 to 0.4375
- gain_mlp: bfloat16 [192], replicated, may hold values from 0.099609375 to 1.8984375
- w_up: bfloat16 [192, 768], replicated, may hold values from -0.4375 to 0.4375
- w_down: bfloat16 [768, 192], replicated, may hold values from -0.21875 to 0.21875
- bias_table: float32 [64, 6, 3312], P('lat'), may hold values from -6 to 6
- index_table: int32 [144, 144], replicated, may hold values from 0 to 3311, as said below
- cotangent: bfloat16 [8, 96, 192, 192], P(None, 'lat', 'lon'), may hold values from -6 to 6
Outputs:
- updated: bfloat16 [8, 96, 192, 192], P(None, 'lat', 'lon')
- d_tokens: bfloat16 [8, 96, 192, 192], P(None, 'lat', 'lon')
- d_gain_attn: float32 [192], replicated
- d_qkv: float32 [192, 576], replicated
- d_proj: float32 [192, 192], replicated
- d_gain_mlp: float32 [192], replicated
- d_up: float32 [192, 768], replicated
- d_down: float32 [768, 192], replicated
- d_bias_table: float32 [64, 6, 3312], P('lat')
Inputs may be any that keep to these rules, and one draw needn't show every extreme that they name: `lat_valid`: 1 on every row but the last 1 to 5 rows, which are 0. `index_table`: every row of the bias table is named by some entry.
All inputs are finite; a program needn't handle non-finite values.
Results may differ from a plain program's by a relative error of at most 0.025.
Values may be sent and summed in bfloat16 or wider, within the bound.
A program may use at most 192 MiB of HBM per device.

v0:
```python
import jax
import jax.numpy as jnp
from jax import lax
from jax.sharding import PartitionSpec as P

WIN_Z = 2
WIN_LAT = 6
WIN_LON = 12
norm_eps = 1e-05


def shifted(value, axis, steps):
    count = lax.axis_size(axis)
    pairs = [(source, (source + steps) % count) for source in range(count)]
    return lax.ppermute(value, axis, pairs)


def product(form, left, right):
    return jnp.einsum(form, left, right, preferred_element_type=jnp.float32)


def layer_norm(inputs, norm_gain):
    inputs = inputs.astype(jnp.float32)
    center = inputs - jnp.mean(inputs, axis=-1, keepdims=True)
    rscale = lax.rsqrt(jnp.mean(center * center, axis=-1, keepdims=True) + norm_eps)
    return center * rscale * norm_gain.astype(jnp.float32)


def norm_back(inputs, norm_gain, incoming):
    inputs = inputs.astype(jnp.float32)
    center = inputs - jnp.mean(inputs, axis=-1, keepdims=True)
    rscale = lax.rsqrt(jnp.mean(center * center, axis=-1, keepdims=True) + norm_eps)
    normed = center * rscale
    scaled = incoming * norm_gain.astype(jnp.float32)
    d_inputs = rscale * (
        scaled
        - jnp.mean(scaled, axis=-1, keepdims=True)
        - normed * jnp.mean(scaled * normed, axis=-1, keepdims=True)
    )
    d_gain = jnp.sum((incoming * normed).reshape(-1, inputs.shape[-1]), axis=0)
    return (d_inputs, d_gain)


def to_windows(grid_field):
    levels, row_count, col_count, channels = grid_field.shape
    blocks = grid_field.reshape(
        levels // WIN_Z,
        WIN_Z,
        row_count // WIN_LAT,
        WIN_LAT,
        col_count // WIN_LON,
        WIN_LON,
        channels,
    )
    blocks = blocks.transpose(0, 2, 4, 1, 3, 5, 6)
    return blocks.reshape(
        levels // WIN_Z,
        row_count // WIN_LAT,
        col_count // WIN_LON,
        WIN_Z * WIN_LAT * WIN_LON,
        channels,
    )


def from_windows(blocks, levels, row_count, col_count):
    channels = blocks.shape[-1]
    blocks = blocks.reshape(
        levels // WIN_Z,
        row_count // WIN_LAT,
        col_count // WIN_LON,
        WIN_Z,
        WIN_LAT,
        WIN_LON,
        channels,
    )
    return blocks.transpose(0, 3, 1, 4, 2, 5, 6).reshape(levels, row_count, col_count, channels)


def window_regions(zone_count, last_band):
    positions = jnp.arange(WIN_Z * WIN_LAT * WIN_LON, dtype=jnp.int32)
    in_depth = positions // (WIN_LAT * WIN_LON)
    in_row = positions // WIN_LON % WIN_LAT
    zone_index = jnp.arange(zone_count, dtype=jnp.int32)[:, None]
    level_part = jnp.where(
        zone_index == zone_count - 1,
        1 + (in_depth[None, :] >= WIN_Z - WIN_Z // 2).astype(jnp.int32),
        0,
    )
    row_part = jnp.where(last_band, 1 + (in_row >= WIN_LAT - WIN_LAT // 2).astype(jnp.int32), 0)
    region = 3 * level_part + row_part[None, :]
    return (region[:, :, None] == region[:, None, :]).astype(jnp.float32)


def into_shifted(grid_field):
    row_half = WIN_LAT // 2
    col_half = WIN_LON // 2
    lower_rows = shifted(grid_field[:, :row_half], "lat", -1)
    grid_field = jnp.concatenate([grid_field[:, row_half:], lower_rows], axis=1)
    next_cols = shifted(grid_field[:, :, :col_half], "lon", -1)
    grid_field = jnp.concatenate([grid_field[:, :, col_half:], next_cols], axis=2)
    return jnp.roll(grid_field, -(WIN_Z // 2), axis=0)


def from_shifted(grid_field):
    row_half = WIN_LAT // 2
    col_half = WIN_LON // 2
    grid_field = jnp.roll(grid_field, WIN_Z // 2, axis=0)
    row_count = grid_field.shape[1]
    col_count = grid_field.shape[2]
    upper_rows = shifted(grid_field[:, row_count - row_half :], "lat", 1)
    grid_field = jnp.concatenate([upper_rows, grid_field[:, : row_count - row_half]], axis=1)
    prev_cols = shifted(grid_field[:, :, col_count - col_half :], "lon", 1)
    return jnp.concatenate([prev_cols, grid_field[:, :, : col_count - col_half]], axis=2)


def attend(windows, w_qkv, w_proj, pos_bias, allowed):
    window_count, places, channels = windows.shape
    head_count = pos_bias.shape[0]
    head_width = channels // head_count
    triple = product("bpc,cd->bpd", windows, w_qkv).astype(jnp.bfloat16)
    parted = triple.reshape(window_count, places, 3, head_count, head_width)
    queries, key_part, values = (parted[:, :, 0], parted[:, :, 1], parted[:, :, 2])
    scores = product("bqhd,bkhd->bhqk", queries, key_part) * head_width ** (-0.5) + pos_bias[None]
    weights = jnp.exp(scores) * allowed[None, None]
    chances = (weights / jnp.sum(weights, axis=-1, keepdims=True)).astype(jnp.bfloat16)
    merged = (
        product("bhqk,bkhd->bqhd", chances, values)
        .astype(jnp.bfloat16)
        .reshape(window_count, places, channels)
    )
    attended = product("bpc,cd->bpd", merged, w_proj).astype(jnp.bfloat16)
    return (attended, triple, chances, merged)


def attend_back(incoming, windows, triple, chances, merged, w_qkv, w_proj):
    window_count, places, channels = windows.shape
    head_count = chances.shape[1]
    head_width = channels // head_count
    d_proj = product("bpc,bpd->cd", merged, incoming)
    d_merged = (
        product("bpd,cd->bpc", incoming, w_proj)
        .astype(jnp.bfloat16)
        .reshape(window_count, places, head_count, head_width)
    )
    parted = triple.reshape(window_count, places, 3, head_count, head_width)
    queries, key_part, values = (parted[:, :, 0], parted[:, :, 1], parted[:, :, 2])
    d_chances = product("bqhd,bkhd->bhqk", d_merged, values)
    d_values = product("bhqk,bqhd->bkhd", chances, d_merged)
    chance_f = chances.astype(jnp.float32)
    d_scores = chance_f * (d_chances - jnp.sum(chance_f * d_chances, axis=-1, keepdims=True))
    scaled = (d_scores * head_width ** (-0.5)).astype(jnp.bfloat16)
    d_queries = product("bhqk,bkhd->bqhd", scaled, key_part)
    d_keys = product("bhqk,bqhd->bkhd", scaled, queries)
    d_triple = (
        jnp.stack([d_queries, d_keys, d_values], axis=2)
        .astype(jnp.bfloat16)
        .reshape(window_count, places, 3 * channels)
    )
    d_qkv = product("bpc,bpd->cd", windows, d_triple)
    d_windows = product("bpd,cd->bpc", d_triple, w_qkv).astype(jnp.bfloat16)
    return (d_windows, d_qkv, d_proj, jnp.sum(d_scores, axis=0))


def table_grad(score_sums, index_flat, entries):
    zone_count, head_count = (score_sums.shape[0], score_sums.shape[1])
    flat_scores = score_sums.reshape(zone_count * head_count, -1).T
    summed = jax.ops.segment_sum(flat_scores, index_flat, num_segments=entries)
    return summed.T.reshape(zone_count, head_count, entries)


def mlp_block(residual, gain_mlp, w_up, w_down):
    second_norm = layer_norm(residual, gain_mlp).astype(jnp.bfloat16)
    hidden_pre = jnp.dot(second_norm, w_up, preferred_element_type=jnp.float32)
    hidden = jax.nn.gelu(hidden_pre).astype(jnp.bfloat16)
    lifted = jnp.dot(hidden, w_down, preferred_element_type=jnp.float32)
    return (second_norm, hidden_pre, hidden, lifted)


def mlp_back(second_norm, hidden_pre, hidden, residual, gain_mlp, w_up, w_down, upstream):
    d_down = jnp.dot(hidden.T, upstream, preferred_element_type=jnp.float32)
    d_hidden = jnp.dot(upstream, w_down.T, preferred_element_type=jnp.float32)
    d_pre = jax.vjp(jax.nn.gelu, hidden_pre)[1](d_hidden)[0].astype(jnp.bfloat16)
    d_up = jnp.dot(second_norm.T, d_pre, preferred_element_type=jnp.float32)
    d_norm = jnp.dot(d_pre, w_up.T, preferred_element_type=jnp.float32)
    d_resid, d_gain = norm_back(residual, gain_mlp, d_norm)
    return (d_resid + upstream.astype(jnp.float32), d_up, d_down, d_gain)


def per_device(
    tokens,
    lat_valid,
    gain_attn,
    w_qkv,
    w_proj,
    gain_mlp,
    w_up,
    w_down,
    bias_table,
    index_table,
    cotangent,
):
    levels, row_count, col_count, channels = tokens.shape
    zone_count = levels // WIN_Z
    places = WIN_Z * WIN_LAT * WIN_LON
    entries = bias_table.shape[2]
    lat_count = lax.axis_size("lat")
    last_band = lax.axis_index("lat") == lat_count - 1
    grad_scale = float(levels * row_count * col_count * lat_count * lax.axis_size("lon")) ** (-0.5)
    keep_rows = (lat_valid > 0)[None, :, None, None]
    inputs = jnp.where(keep_rows, tokens, jnp.zeros_like(tokens))
    upstream = jnp.where(keep_rows, cotangent, jnp.zeros_like(cotangent))
    index_flat = index_table.reshape(-1)
    pos_bias = jnp.take(bias_table, index_flat, axis=2).reshape(zone_count, -1, places, places)
    allowed = window_regions(zone_count, last_band)

    def forward_pass(block_inputs):
        first_norm = layer_norm(block_inputs, gain_attn).astype(jnp.bfloat16)
        windows = to_windows(into_shifted(first_norm))[:, 0]

        def zone_forward(zone_parts):
            return attend(zone_parts[0], w_qkv, w_proj, zone_parts[1], zone_parts[2])

        attended, triple, chances, merged = lax.map(zone_forward, (windows, pos_bias, allowed))
        attn_out = from_shifted(from_windows(attended[:, None], levels, row_count, col_count))
        residual = (block_inputs.astype(jnp.float32) + attn_out.astype(jnp.float32)).astype(
            jnp.bfloat16
        )
        second_norm, hidden_pre, hidden, lifted = mlp_block(
            residual.reshape(-1, channels), gain_mlp, w_up, w_down
        )
        result = jnp.where(
            keep_rows, residual.astype(jnp.float32) + lifted.reshape(residual.shape), 0.0
        ).astype(jnp.bfloat16)
        return (
            result,
            (windows, triple, chances, merged, residual, second_norm, hidden_pre, hidden),
        )

    updated, kept_state = forward_pass(inputs)
    inputs_again, upstream = lax.optimization_barrier((inputs, upstream))
    kept_state = forward_pass(inputs_again)[1]
    windows, triple, chances, merged, residual, second_norm, hidden_pre, hidden = kept_state
    d_resid, d_up, d_down, d_gain_mlp = mlp_back(
        second_norm,
        hidden_pre,
        hidden,
        residual.reshape(-1, channels),
        gain_mlp,
        w_up,
        w_down,
        upstream.reshape(-1, channels),
    )
    d_up = d_up * grad_scale
    d_down = d_down * grad_scale
    d_gain_mlp = d_gain_mlp * grad_scale
    d_residual = d_resid.reshape(tokens.shape)
    d_incoming = to_windows(into_shifted(d_residual.astype(jnp.bfloat16)))[:, 0]

    def zone_back(zone_parts):
        return attend_back(
            zone_parts[0], zone_parts[1], zone_parts[2], zone_parts[3], zone_parts[4], w_qkv, w_proj
        )

    d_wins, d_qkv_z, d_proj_z, d_score_z = lax.map(
        zone_back, (d_incoming, windows, triple, chances, merged)
    )
    d_table = lax.psum(
        (table_grad(d_score_z, index_flat, entries) * grad_scale).astype(jnp.bfloat16), "lon"
    ).astype(jnp.float32)
    d_first = from_shifted(from_windows(d_wins[:, None], levels, row_count, col_count))
    d_inputs, d_gain_attn = norm_back(inputs, gain_attn, d_first.astype(jnp.float32))
    d_tokens = jnp.where(keep_rows, d_residual + d_inputs, 0.0).astype(jnp.bfloat16)
    d_qkv = jnp.sum(d_qkv_z, axis=0) * grad_scale
    d_proj = jnp.sum(d_proj_z, axis=0) * grad_scale
    d_gain_attn = d_gain_attn * grad_scale
    d_gain_attn, d_qkv, d_proj, d_gain_mlp, d_up, d_down = lax.psum(
        (d_gain_attn, d_qkv, d_proj, d_gain_mlp, d_up, d_down), ("lat", "lon")
    )
    return (updated, d_tokens, d_gain_attn, d_qkv, d_proj, d_gain_mlp, d_up, d_down, d_table)


def solution(mesh):
    in_specs = (
        P(None, "lat", "lon", None),
        P("lat"),
        P(),
        P(),
        P(),
        P(),
        P(),
        P(),
        P("lat", None, None),
        P(),
        P(None, "lat", "lon", None),
    )
    out_specs = (
        P(None, "lat", "lon", None),
        P(None, "lat", "lon", None),
        P(),
        P(),
        P(),
        P(),
        P(),
        P(),
        P("lat", None, None),
    )
    return jax.shard_map(
        per_device, mesh=mesh, in_specs=in_specs, out_specs=out_specs, check_vma=False
    )
```

profile of v0, /device:TPU:1, one launch (start us, length us, event | category | flops | bytes accessed | tf_op | source)
XLA Modules:
  0.0 720.1 jit_solution(3983639342740741264)
XLA Ops:
  15.3 4.8 copy.206
  20.4 60.8 %gather_fusion = f32[20736,4,6]{2,1,0:T(4,128)} fusion(f32[4,6,3312]{1,0,2:T(4,128)} %copy.206, s32[21504]{0:T(1024)S(1)} %pad_clamp_fusion), kind=kCustom, calls=%fused_computation | custom fusion | bytes 4064256 | tf_op jit(solution)/shard_map/jit(_take)/gather | solution.py:213
  81.1 42.5 %copy.257 = f32[4,6,144,144]{3,2,0,1:T(8,128)} copy(f32[4,6,144,144]{1,0,3,2:T(4,128)} %bitcast.340) | data formatting | bytes 3981312 | tf_op jit(solution)/shard_map/jit(_take)/gather | solution.py:213
  123.6 4.2 broadcast_select_fusion
  127.8 5.6 copy.209
  134.5 6.4 collective-permute-start.5
  146.4 44.5 %while.43 = (s32[]{:T(128)}, bf16[4,2,144,192]{3,1,2,0:T(2,128)(2,1)}, bf16[4,2,144,576]{3,2,1,0:T(8,128)(2,1)}, bf16[4,2,6,144,144]{3,4,2,1,0:T(8,128)(2,1)}, b...) while((s32[]{:T(128)}, ...), condition=%wide.region_11.12_spmd, body=%wide.region_9.11_spmd.sunk | while | flops 118307664 | bytes 7928437 | solution.py:223
  151.7 2.9 bitcast_dynamic-update-slice_fusion.5
  162.8 2.9 bitcast_dynamic-update-slice_fusion.5
  173.9 2.9 bitcast_dynamic-update-slice_fusion.5
  185.1 2.8 bitcast_dynamic-update-slice_fusion.5
  193.5 3.1 collective-permute-start.6
  197.0 3.2 collective-permute-done.6
  203.7 6.1 collective-permute-done.7
  215.8 2.6 fusion.46
  220.6 6.6 collective-permute-start.8
  236.0 90.7 %while.44 = (s32[]{:T(128)}, bf16[4,2,144,192]{3,1,2,0:T(2,128)(2,1)}, f32[4,192,576]{2,1,0:T(8,128)}, f32[4,192,192]{2,1,0:T(8,128)}, f32[4,6,144,144]{3,2,1,0:...) while((s32[]{:T(128)}, ...), condition=%wide.region_19.20_spmd, body=%wide.region_16.19_spmd.sunk | while | flops 238870512 | bytes 34235124 | solution.py:264
  248.0 2.7 convolution_bitcast_fusion.9
  270.7 2.8 convolution_bitcast_fusion.9
  293.4 2.8 convolution_bitcast_fusion.9
  316.1 2.7 convolution_bitcast_fusion.9
  329.9 2.6 collective-permute-start.10
  333.1 5.0 reshape.376
  338.1 6.9 copy.242
  345.0 112.8 %scatter_custom_fusion = f32[3312,24]{1,0:T(8,128)S(1)} fusion(s32[20736]{0:T(1024)} %reshape.389, f32[20736,24]{1,0:T(8,128)} %copy.242, f32[]{:T(128)} %constant.143.clone.1), kind=kCustom, calls=%fused_computation.155 | custom fusion | flops 497664 | bytes 318464 | tf_op jit(solution)/shard_map/scatter-add | solution.py:167
  470.7 2.7 collective-permute-start
  474.3 3.8 collective-permute-done
  478.1 3.9 collective-permute-start.1
  487.4 29.3 %while.42 = (s32[]{:T(128)}, bf16[4,2,144,192]{3,1,2,0:T(2,128)(2,1)}, bf16[4,2,144,192]{3,1,2,0:T(2,128)(2,1)}, bf16[192,576]{1,0:T(8,128)(2,1)S(1)}, f32[4,6,1...) while((s32[]{:T(128)}, bf16[4,2,144,192]{3,1,2,0:T(2,128)(2,1)}, ...), condition=%wide.region_4.5_spmd, body=%wide.region_2.4_spmd.sunk | while | flops 118307664 | bytes 9529953 | solution.py:223
  522.0 24.7 %all-reduce.5.cloned.1.call-done = bf16[4,6,3312]{2,1,0:T(8,128)(2,1)} async-done(((bf16[4,6,3312]{2,1,0:T(8,128)(2,1)}), bf16[4,6,3312]{2,1,0:T(8,128)(2,1)}) %all-reduce.5.cloned.1.call-update) | async-done | bytes 158992 | tf_op jit(solution)/shard_map/psum | solution.py:267
  550.2 69.6 %all-reduce = (f32[192]{0:T(256)}, f32[192]{0:T(256)}) all-reduce(f32[192]{0:T(256)S(1)} %broadcast_multiply_fusion.11, f32[192]{0:T(256)S(1)} %copy-done.28), channel_id=1, replica_groups=mesh['lat'=16,'lon'=8] {'lat','lon'}, use_global_device_ids=true, to_apply=%region_23.24 | all-reduce | flops 384 | bytes 3072 | tf_op jit(solution)/shard_map/psum | solution.py:276
  624.7 83.1 %all-reduce.7.cloned.1.call-done = (f32[192,576]{1,0:T(8,128)}, f32[192,192]{1,0:T(8,128)}, f32[192,768]{1,0:T(8,128)}, f32[768,192]{0,1:T(8,128)}) async-done(((f32[192,576]{1,0:T(8,128)}, f32[192,192]{1,0:T(8,128)}, f32[192,768]{1,0:T(8,128)}, f32[768,192]{0,1:T(8,128)}), (f32[192,576]{1,0:T(8,128)}, f32[192,192]{1,0:T(8,128)}, f32[192,768]{1,0:T(8,128)}, ...) | async-done | bytes 1769488 | tf_op jit(solution)/shard_map/psum | solution.py:276
  (371 shorter events, 220.9 us)
Async XLA Ops:
  7.2 205.5 %copy-start = (bf16[192,768]{1,0:T(8,128)(2,1)S(1)}, bf16[192,768]{1,0:T(8,128)(2,1)}, u32[]{:S(2)}) copy-start(bf16[192,768]{1,0:T(8,128)(2,1)} %param.23) | copy-start | bytes 884740
  7.2 539.5 %all-reduce.5.cloned.1.call-start = ((), (), s32[]{:S(2)}) async-start(), calls=%async_computation | async-start | bytes 425984 | tf_op jit(solution)/shard_map/psum | solution.py:267
  7.9 5.1 copy-start.31
  10.0 199.8 %copy-start.2 = (bf16[8,6,24,192]{3,0,2,1:T(8,128)(2,1)}, bf16[8,6,24,192]{3,0,2,1:T(8,128)(2,1)S(1)}, u32[]{:S(2)}) copy-start(bf16[8,6,24,192]{3,0,2,1:T(8,128)(2,1)S(1)} %get-tuple-element.169) | copy-start | bytes 1327108
  13.5 121.0 %collective-permute-start.4 = (bf16[8,3,24,192]{3,0,2,1:T(8,128)(2,1)S(1)}, bf16[8,3,24,192]{3,0,2,1:T(8,128)(2,1)S(1)}, u32[]{:S(2)}, u32[]{:S(2)}) collective-permute-start(bf16[8,3,24,192]{3,0,2,1:T(8,128)(2,1)S(1)} %get-tuple-element.401), channel_id=1, source_target_pairs={{0,120},{8,0},{16,8},{24,16},{32,24},{40,32},{48,40},{56,48},{64,5... | collective-permute-start | bytes 663560 | tf_op jit(solution)/shard_map/ppermute | solution.py:15
  134.5 8.5 %collective-permute-start.5 = (bf16[8,6,6,192]{3,0,2,1:T(8,128)(2,1)S(1)}, bf16[8,6,6,192]{3,0,2,1:T(8,128)(2,1)S(1)}, u32[]{:S(2)}, u32[]{:S(2)}) collective-permute-start(bf16[8,6,6,192]{3,0,2,1:T(8,128)(2,1)S(1)} %pad_maximum_fusion.12), channel_id=1, source_target_pairs={{0,7},{1,0},{2,1},{3,2},{4,3},{5,4},{6,5},{7,6},{8,15},{9,8},{10,9... | collective-permute-start | bytes 331784 | tf_op jit(solution)/shard_map/ppermute | solution.py:15
  190.9 5.7 copy-start.27
  193.3 9.3 %copy-start.32 = (bf16[192]{0:T(256)(128)(2,1)S(1)}, bf16[192]{0:T(256)(128)(2,1)}, u32[]{:S(2)}) copy-start(bf16[192]{0:T(256)(128)(2,1)} %param.22) | copy-start | bytes 1156
  193.3 9.3 %copy-start.13 = (bf16[8,6,24,192]{3,0,2,1:T(8,128)(2,1)S(1)}, bf16[8,6,24,192]{3,0,2,1:T(8,128)(2,1)}, u32[]{:S(2)}) copy-start(bf16[8,6,24,192]{3,0,2,1:T(8,128)(2,1)} %copy_select_fusion) | copy-start | bytes 1327108
  193.5 6.8 collective-permute-start.6
  196.6 6.0 copy-start.20
  201.0 8.9 %collective-permute-start.7 = (bf16[8,6,6,192]{3,0,2,1:T(8,128)(2,1)}, bf16[8,6,6,192]{3,0,2,1:T(8,128)(2,1)}, u32[]{:S(2)}, u32[]{:S(2)}) collective-permute-start(bf16[8,6,6,192]{3,0,2,1:T(8,128)(2,1)} %pad_maximum_fusion.11), channel_id=1, source_target_pairs={{0,1},{1,2},{2,3},{3,4},{4,5},{5,6},{6,7},{7,0},{8,9},{9,10},{10,1... | collective-permute-start | bytes 331784 | tf_op jit(solution)/shard_map/ppermute | solution.py:15
  220.4 8.1 %copy-start.6 = (f32[1152,192]{1,0:T(8,128)}, f32[1152,192]{1,0:T(8,128)S(1)}, u32[]{:S(2)}) copy-start(f32[1152,192]{1,0:T(8,128)S(1)} %copy.231) | copy-start | bytes 2654212
  220.4 6.7 copy-start.16
  220.6 8.0 %collective-permute-start.8 = (bf16[8,3,24,192]{3,2,1,0:T(8,128)(2,1)S(1)}, bf16[8,3,24,192]{3,2,1,0:T(8,128)(2,1)S(1)}, u32[]{:S(2)}, u32[]{:S(2)}) collective-permute-start(bf16[8,3,24,192]{3,2,1,0:T(8,128)(2,1)S(1)} %get-tuple-element.399), channel_id=1, source_target_pairs={{0,120},{8,0},{16,8},{24,16},{32,24},{40,32},{48,40},{56,48},{64,5... | collective-permute-start | bytes 663560 | tf_op jit(solution)/shard_map/ppermute | solution.py:15
  228.6 4.8 collective-permute-start.9
  253.4 5.2 copy-start.10
  276.1 5.2 copy-start.10
  298.9 5.2 copy-start.10
  321.5 5.2 copy-start.10
  329.0 128.9 %copy-start.11 = (bf16[1,6,24,192]{3,0,2,1:T(2,128)(2,1)}, bf16[1,6,24,192]{3,0,2,1:T(2,128)(2,1)S(1)}, u32[]{:S(2)}) copy-start(bf16[1,6,24,192]{3,0,2,1:T(2,128)(2,1)S(1)} %slice.212) | copy-start | bytes 165892
  329.9 128.0 %collective-permute-start.10 = (bf16[8,3,24,192]{3,0,2,1:T(8,128)(2,1)}, bf16[8,3,24,192]{3,0,2,1:T(8,128)(2,1)S(1)}, u32[]{:S(2)}, u32[]{:S(2)}) collective-permute-start(bf16[8,3,24,192]{3,0,2,1:T(8,128)(2,1)} %fusion.102), channel_id=1, source_target_pairs={{0,8},{8,16},{16,24},{24,32},{32,40},{40,48},{48,56},{56,64},{64,7... | collective-permute-start | bytes 663560 | tf_op jit(solution)/shard_map/ppermute | solution.py:15
  458.6 8.2 %collective-permute-start.11 = (bf16[8,6,6,192]{3,0,2,1:T(8,128)(2,1)}, bf16[8,6,6,192]{3,0,2,1:T(8,128)(2,1)}, u32[]{:S(2)}, u32[]{:S(2)}) collective-permute-start(bf16[8,6,6,192]{3,0,2,1:T(8,128)(2,1)} %pad_maximum_fusion.10), channel_id=1, source_target_pairs={{0,1},{1,2},{2,3},{3,4},{4,5},{5,6},{6,7},{7,0},{8,9},{9,10},{10,1... | collective-permute-start | bytes 331784 | tf_op jit(solution)/shard_map/ppermute | solution.py:15
  461.4 5.4 copy-start.3
  461.5 5.4 copy-start.12
  466.2 241.7 %all-reduce.7.cloned.1.call-start = ((), (), s32[]{:S(2)}) async-start(), calls=%async_computation.1 | async-start | bytes 3735552 | tf_op jit(solution)/shard_map/psum | solution.py:276
  470.7 7.4 %collective-permute-start = (bf16[8,3,24,192]{3,0,2,1:T(8,128)(2,1)S(1)}, bf16[8,3,24,192]{3,0,2,1:T(8,128)(2,1)S(1)}, u32[]{:S(2)}, u32[]{:S(2)}) collective-permute-start(bf16[8,3,24,192]{3,0,2,1:T(8,128)(2,1)S(1)} %get-tuple-element.403), channel_id=1, source_target_pairs={{0,120},{8,0},{16,8},{24,16},{32,24},{40,32},{48,40},{56,48},{64,5... | collective-permute-start | bytes 663560 | tf_op jit(solution)/shard_map/ppermute | solution.py:15
  478.1 6.0 collective-permute-start.1
  519.3 29.1 %collective-permute-start.2 = (bf16[8,3,24,192]{3,0,2,1:T(8,128)(2,1)S(1)}, bf16[8,3,24,192]{3,0,2,1:T(8,128)(2,1)S(1)}, u32[]{:S(2)}, u32[]{:S(2)}) collective-permute-start(bf16[8,3,24,192]{3,0,2,1:T(8,128)(2,1)S(1)} %fusion.104), channel_id=1, source_target_pairs={{0,8},{8,16},{16,24},{24,32},{32,40},{40,48},{48,56},{56,64},{64,7... | collective-permute-start | bytes 663560 | tf_op jit(solution)/shard_map/ppermute | solution.py:15
  521.9 27.3 %copy-start.14 = (bf16[8,6,24,192]{3,0,2,1:T(8,128)(2,1)S(1)}, bf16[8,6,24,192]{3,0,2,1:T(8,128)(2,1)}, u32[]{:S(2)}) copy-start(bf16[8,6,24,192]{3,0,2,1:T(8,128)(2,1)} %get-tuple-element.396) | copy-start | bytes 1327108
  522.0 28.2 %copy-start.28 = (f32[192]{0:T(256)S(1)}, f32[192]{0:T(256)}, u32[]{:S(2)}) copy-start(f32[192]{0:T(256)} %broadcast_multiply_fusion.10) | copy-start | bytes 2308
  548.4 71.3 %collective-permute-start.3 = (bf16[8,6,6,192]{3,0,2,1:T(8,128)(2,1)S(1)}, bf16[8,6,6,192]{3,0,2,1:T(8,128)(2,1)S(1)}, u32[]{:S(2)}, u32[]{:S(2)}) collective-permute-start(bf16[8,6,6,192]{3,0,2,1:T(8,128)(2,1)S(1)} %pad_maximum_fusion.13), channel_id=1, source_target_pairs={{0,1},{1,2},{2,3},{3,4},{4,5},{5,6},{6,7},{7,0},{8,9},{9,10},{10,1... | collective-permute-start | bytes 331784 | tf_op jit(solution)/shard_map/ppermute | solution.py:15
  (27 other events, 57.1 us)
Sparse Core Ops, SparseCore 0:
  466.3 80.3 all-reduce.4
  553.6 154.2 all-reduce.6
where the time goes:
time: 731 us; the launch traced here: 720 us
  local copies, waits for them, and re-layouts  221 us (30%)
  other arithmetic  157 us (21%)
  waiting for transfers between devices  128 us (18%)
  matrix products  95.9 us (13%)
  blocking collectives  69.6 us (10%)
  starting transfers between devices  32 us (4%)
  between operations  15 us (2%)
    scatter-add x1, other arithmetic, table_grad(): summed = jax.ops.segment_sum(flat_scores, index_flat, num_segments=entries)  113 us
    gather x2, local copies, waits for them, and re-layouts, per_device(): jnp.take(bias_table, index_flat, axis=2)  103 us
    psum x1, waiting for transfers between devices, per_device(): lax.psum((d_gain_attn, d_qkv, d_proj, d_gain_mlp, d_up, d_down), ('lat',...  83.1 us
    dot_general x60, matrix products, product(): return jnp.einsum(form, left, right, preferred_element_type=jnp.float32)  74.8 us
    psum x1, blocking collectives, per_device(): lax.psum((d_gain_attn, d_qkv, d_proj, d_gain_mlp, d_up, d_down), ('lat',...  69.6 us
    ppermute x12, starting transfers between devices, shifted(): return lax.ppermute(value, axis, pairs)  31.9 us
    psum x1, waiting for transfers between devices, per_device(): lax.psum((table_grad(d_score_z, index_flat, entries) * grad_scale).astype...  24.7 us
    ppermute x12, waiting for transfers between devices, shifted(): return lax.ppermute(value, axis, pairs)  20.4 us
  transfers between devices with their start and end apart: 14, of which 9 were waited for; matrix products, arithmetic and copies ran while one was open for 42% of the time, Pallas kernels for 0%

commit v1 on v0

--- a/solution.py
+++ b/solution.py
@@ -264,8 +264,11 @@
     d_wins, d_qkv_z, d_proj_z, d_score_z = lax.map(
         zone_back, (d_incoming, windows, triple, chances, merged)
     )
-    d_table = lax.psum(
-        (table_grad(d_score_z, index_flat, entries) * grad_scale).astype(jnp.bfloat16), "lon"
+    d_table = jnp.sum(
+        lax.all_gather(
+            (table_grad(d_score_z, index_flat, entries) * grad_scale).astype(jnp.bfloat16), "lon"
+        ),
+        axis=0,
     ).astype(jnp.float32)
     d_first = from_shifted(from_windows(d_wins[:, None], levels, row_count, col_count))
     d_inputs, d_gain_attn = norm_back(inputs, gain_attn, d_first.astype(jnp.float32))

time: 731 us -> 702 us (0.960)
  waiting for transfers between devices: 128 us -> 93.8 us
    psum x1 -> x0, waiting for transfers between devices: 24.7 us -> none  [per_device(): lax.psum((table_grad(d_score_z, index_flat, entries) * grad_scale).astype...]
    psum x1, waiting for transfers between devices: 83.1 us -> 69.7 us  [per_device(): lax.psum((d_gain_attn, d_qkv, d_proj, d_gain_mlp, d_up, d_down), ('lat',...]
  transfers between devices with their start and end apart: 14 -> 14, of which waited for: 9 -> 9; matrix products, arithmetic and copies ran while one was open for 42% -> 44% of each run, Pallas kernels for 0% -> 0%
where the time goes in v1:
time: 702 us; the launch traced here: 691 us
  local copies, waits for them, and re-layouts  221 us (31%)
  other arithmetic  159 us (23%)
  matrix products  95.9 us (14%)
  waiting for transfers between devices  93.8 us (13%)
  blocking collectives  72.7 us (10%)
  starting transfers between devices  31.4 us (4%)
  between operations  16.5 us (2%)
    scatter-add x1, other arithmetic, table_grad(): summed = jax.ops.segment_sum(flat_scores, index_flat, num_segments=entries)  113 us
    gather x2, local copies, waits for them, and re-layouts, per_device(): jnp.take(bias_table, index_flat, axis=2)  103 us
    dot_general x60, matrix products, product(): return jnp.einsum(form, left, right, preferred_element_type=jnp.float32)  74.8 us
    psum x1, blocking collectives, per_device(): lax.psum((d_gain_attn, d_qkv, d_proj, d_gain_mlp, d_up, d_down), ('lat',...  72.7 us
    psum x1, waiting for transfers between devices, per_device(): lax.psum((d_gain_attn, d_qkv, d_proj, d_gain_mlp, d_up, d_down), ('lat',...  69.7 us
    ppermute x12, starting transfers between devices, shifted(): return lax.ppermute(value, axis, pairs)  31.3 us
    ppermute x12, waiting for transfers between devices, shifted(): return lax.ppermute(value, axis, pairs)  24 us
    dynamic_update_slice x8, local copies, waits for them, and re-layouts, per_device(): lax.map(zone_back, (d_incoming, windows, triple, chances, merged))  14.4 us
  transfers between devices with their start and end apart: 14, of which 9 were waited for; matrix products, arithmetic and copies ran while one was open for 44% of the time, Pallas kernels for 0%

profile of v1, /device:TPU:1, one launch (start us, length us, event | category | flops | bytes accessed | tf_op | source)
XLA Modules:
  0.0 690.8 jit_solution(2633843191787550290)
XLA Ops:
  16.1 4.8 copy.206
  21.2 60.8 %gather_fusion = f32[20736,4,6]{2,1,0:T(4,128)} fusion(f32[4,6,3312]{1,0,2:T(4,128)} %copy.206, s32[21504]{0:T(1024)S(1)} %pad_clamp_fusion), kind=kCustom, calls=%fused_computation | custom fusion | bytes 4064256 | tf_op jit(solution)/shard_map/jit(_take)/gather | solution.py:213
  82.0 42.5 %copy.259 = f32[4,6,144,144]{3,2,0,1:T(8,128)} copy(f32[4,6,144,144]{1,0,3,2:T(4,128)} %bitcast.340) | data formatting | bytes 3981312 | tf_op jit(solution)/shard_map/jit(_take)/gather | solution.py:213
  124.5 4.2 broadcast_select_fusion
  128.7 5.6 copy.209
  135.3 6.4 collective-permute-start.5
  147.2 44.5 %while.43 = (s32[]{:T(128)}, bf16[4,2,144,192]{3,1,2,0:T(2,128)(2,1)}, bf16[4,2,144,576]{3,2,1,0:T(8,128)(2,1)}, bf16[4,2,6,144,144]{3,4,2,1,0:T(8,128)(2,1)}, b...) while((s32[]{:T(128)}, ...), condition=%wide.region_11.12_spmd, body=%wide.region_9.11_spmd.sunk | while | flops 118307664 | bytes 7928437 | solution.py:223
  152.5 2.9 bitcast_dynamic-update-slice_fusion.5
  163.7 2.9 bitcast_dynamic-update-slice_fusion.5
  174.8 2.9 bitcast_dynamic-update-slice_fusion.5
  185.9 2.8 bitcast_dynamic-update-slice_fusion.5
  194.3 3.1 collective-permute-start.6
  197.9 3.2 collective-permute-done.6
  204.5 6.1 collective-permute-done.7
  216.6 2.6 fusion.46
  221.4 6.6 collective-permute-start.8
  236.8 90.7 %while.44 = (s32[]{:T(128)}, bf16[4,2,144,192]{3,1,2,0:T(2,128)(2,1)}, f32[4,192,576]{2,1,0:T(8,128)}, f32[4,192,192]{2,1,0:T(8,128)}, f32[4,6,144,144]{3,2,1,0:...) while((s32[]{:T(128)}, ...), condition=%wide.region_19.20_spmd, body=%wide.region_16.19_spmd.sunk | while | flops 238870512 | bytes 34235124 | solution.py:264
  248.8 2.7 convolution_bitcast_fusion.9
  271.5 2.8 convolution_bitcast_fusion.9
  294.3 2.8 convolution_bitcast_fusion.9
  316.9 2.7 convolution_bitcast_fusion.9
  330.7 2.6 collective-permute-start.10
  333.9 5.0 reshape.389
  338.9 6.9 %copy.242 = f32[20736,24]{1,0:T(8,128)} copy(f32[20736,24]{0,1:T(8,128)} %bitcast.363) | data formatting | bytes 3981312 | tf_op jit(solution)/shard_map/transpose | solution.py:166
  345.9 112.8 %scatter_custom_fusion = f32[3312,24]{1,0:T(8,128)S(1)} fusion(s32[20736]{0:T(1024)} %reshape.402, f32[20736,24]{1,0:T(8,128)} %copy.242, f32[]{:T(128)} %constant.144.clone.1), kind=kCustom, calls=%fused_computation.155 | custom fusion | flops 497664 | bytes 318464 | tf_op jit(solution)/shard_map/scatter-add | solution.py:167
  471.5 2.7 collective-permute-start
  475.1 3.8 collective-permute-done
  478.9 4.0 collective-permute-start.1
  488.4 29.3 %while.42 = (s32[]{:T(128)}, bf16[4,2,144,192]{3,1,2,0:T(2,128)(2,1)}, bf16[4,2,144,192]{3,1,2,0:T(2,128)(2,1)}, bf16[192,576]{1,0:T(8,128)(2,1)S(1)}, f32[4,6,1...) while((s32[]{:T(128)}, bf16[4,2,144,192]{3,1,2,0:T(2,128)(2,1)}, ...), condition=%wide.region_4.5_spmd, body=%wide.region_2.4_spmd.sunk | while | flops 118307664 | bytes 9529953 | solution.py:223
  522.9 3.7 collective-permute-done.2
  527.8 72.7 %all-reduce = (f32[192]{0:T(256)}, f32[192]{0:T(256)}) all-reduce(f32[192]{0:T(256)S(1)} %broadcast_multiply_fusion.11, f32[192]{0:T(256)S(1)} %copy-done.28), channel_id=1, replica_groups=mesh['lat'=16,'lon'=8] {'lat','lon'}, use_global_device_ids=true, to_apply=%region_23.24 | all-reduce | flops 384 | bytes 3072 | tf_op jit(solution)/shard_map/psum | solution.py:279
  608.3 69.7 %all-reduce.4.cloned.1.call-done = (f32[192,576]{1,0:T(8,128)}, f32[192,192]{1,0:T(8,128)}, f32[192,768]{1,0:T(8,128)}, f32[768,192]{0,1:T(8,128)}) async-done(((f32[192,576]{1,0:T(8,128)}, f32[192,192]{1,0:T(8,128)}, f32[192,768]{1,0:T(8,128)}, f32[768,192]{0,1:T(8,128)}), (f32[192,576]{1,0:T(8,128)}, f32[192,192]{1,0:T(8,128)}, f32[192,768]{1,0:T(8,128)}, ...) | async-done | bytes 1769488 | tf_op jit(solution)/shard_map/psum | solution.py:279
  (374 shorter events, 221.3 us)
Async XLA Ops:
  8.0 205.5 %copy-start = (bf16[192,768]{1,0:T(8,128)(2,1)S(1)}, bf16[192,768]{1,0:T(8,128)(2,1)}, u32[]{:S(2)}) copy-start(bf16[192,768]{1,0:T(8,128)(2,1)} %param.23) | copy-start | bytes 884740
  8.0 597.4 %all-gather.2.cloned.1.call-start = ((), (), s32[]{:S(2)}) async-start(), calls=%async_computation | async-start | bytes 1437696 | tf_op jit(solution)/shard_map/all_gather | solution.py:268
  8.8 5.1 copy-start.31
  10.8 199.8 %copy-start.2 = (bf16[8,6,24,192]{3,0,2,1:T(8,128)(2,1)}, bf16[8,6,24,192]{3,0,2,1:T(8,128)(2,1)S(1)}, u32[]{:S(2)}) copy-start(bf16[8,6,24,192]{3,0,2,1:T(8,128)(2,1)S(1)} %get-tuple-element.169) | copy-start | bytes 1327108
  14.3 121.0 %collective-permute-start.4 = (bf16[8,3,24,192]{3,0,2,1:T(8,128)(2,1)S(1)}, bf16[8,3,24,192]{3,0,2,1:T(8,128)(2,1)S(1)}, u32[]{:S(2)}, u32[]{:S(2)}) collective-permute-start(bf16[8,3,24,192]{3,0,2,1:T(8,128)(2,1)S(1)} %get-tuple-element.401), channel_id=1, source_target_pairs={{0,120},{8,0},{16,8},{24,16},{32,24},{40,32},{48,40},{56,48},{64,5... | collective-permute-start | bytes 663560 | tf_op jit(solution)/shard_map/ppermute | solution.py:15
  135.3 8.5 %collective-permute-start.5 = (bf16[8,6,6,192]{3,0,2,1:T(8,128)(2,1)S(1)}, bf16[8,6,6,192]{3,0,2,1:T(8,128)(2,1)S(1)}, u32[]{:S(2)}, u32[]{:S(2)}) collective-permute-start(bf16[8,6,6,192]{3,0,2,1:T(8,128)(2,1)S(1)} %pad_maximum_fusion.12), channel_id=1, source_target_pairs={{0,7},{1,0},{2,1},{3,2},{4,3},{5,4},{6,5},{7,6},{8,15},{9,8},{10,9... | collective-permute-start | bytes 331784 | tf_op jit(solution)/shard_map/ppermute | solution.py:15
  191.7 5.7 copy-start.27
  194.1 9.3 %copy-start.32 = (bf16[192]{0:T(256)(128)(2,1)S(1)}, bf16[192]{0:T(256)(128)(2,1)}, u32[]{:S(2)}) copy-start(bf16[192]{0:T(256)(128)(2,1)} %param.22) | copy-start | bytes 1156
  194.1 9.3 %copy-start.13 = (bf16[8,6,24,192]{3,0,2,1:T(8,128)(2,1)S(1)}, bf16[8,6,24,192]{3,0,2,1:T(8,128)(2,1)}, u32[]{:S(2)}) copy-start(bf16[8,6,24,192]{3,0,2,1:T(8,128)(2,1)} %copy_select_fusion) | copy-start | bytes 1327108
  194.3 6.8 collective-permute-start.6
  197.4 6.0 copy-start.20
  201.8 8.9 %collective-permute-start.7 = (bf16[8,6,6,192]{3,0,2,1:T(8,128)(2,1)}, bf16[8,6,6,192]{3,0,2,1:T(8,128)(2,1)}, u32[]{:S(2)}, u32[]{:S(2)}) collective-permute-start(bf16[8,6,6,192]{3,0,2,1:T(8,128)(2,1)} %pad_maximum_fusion.11), channel_id=1, source_target_pairs={{0,1},{1,2},{2,3},{3,4},{4,5},{5,6},{6,7},{7,0},{8,9},{9,10},{10,1... | collective-permute-start | bytes 331784 | tf_op jit(solution)/shard_map/ppermute | solution.py:15
  221.3 8.1 %copy-start.6 = (f32[1152,192]{1,0:T(8,128)}, f32[1152,192]{1,0:T(8,128)S(1)}, u32[]{:S(2)}) copy-start(f32[1152,192]{1,0:T(8,128)S(1)} %copy.231) | copy-start | bytes 2654212
  221.3 6.7 copy-start.16
  221.4 8.0 %collective-permute-start.8 = (bf16[8,3,24,192]{3,2,1,0:T(8,128)(2,1)S(1)}, bf16[8,3,24,192]{3,2,1,0:T(8,128)(2,1)S(1)}, u32[]{:S(2)}, u32[]{:S(2)}) collective-permute-start(bf16[8,3,24,192]{3,2,1,0:T(8,128)(2,1)S(1)} %get-tuple-element.399), channel_id=1, source_target_pairs={{0,120},{8,0},{16,8},{24,16},{32,24},{40,32},{48,40},{56,48},{64,5... | collective-permute-start | bytes 663560 | tf_op jit(solution)/shard_map/ppermute | solution.py:15
  229.4 4.8 collective-permute-start.9
  254.2 5.2 copy-start.10
  277.0 5.2 copy-start.10
  299.7 5.2 copy-start.10
  322.3 5.2 copy-start.10
  329.8 128.9 %copy-start.11 = (bf16[1,6,24,192]{3,0,2,1:T(2,128)(2,1)}, bf16[1,6,24,192]{3,0,2,1:T(2,128)(2,1)S(1)}, u32[]{:S(2)}) copy-start(bf16[1,6,24,192]{3,0,2,1:T(2,128)(2,1)S(1)} %slice.212) | copy-start | bytes 165892
  330.7 128.0 %collective-permute-start.10 = (bf16[8,3,24,192]{3,0,2,1:T(8,128)(2,1)}, bf16[8,3,24,192]{3,0,2,1:T(8,128)(2,1)S(1)}, u32[]{:S(2)}, u32[]{:S(2)}) collective-permute-start(bf16[8,3,24,192]{3,0,2,1:T(8,128)(2,1)} %fusion.102), channel_id=1, source_target_pairs={{0,8},{8,16},{16,24},{24,32},{32,40},{40,48},{48,56},{56,64},{64,7... | collective-permute-start | bytes 663560 | tf_op jit(solution)/shard_map/ppermute | solution.py:15
  459.5 8.2 %collective-permute-start.11 = (bf16[8,6,6,192]{3,0,2,1:T(8,128)(2,1)}, bf16[8,6,6,192]{3,0,2,1:T(8,128)(2,1)}, u32[]{:S(2)}, u32[]{:S(2)}) collective-permute-start(bf16[8,6,6,192]{3,0,2,1:T(8,128)(2,1)} %pad_maximum_fusion.10), channel_id=1, source_target_pairs={{0,1},{1,2},{2,3},{3,4},{4,5},{5,6},{6,7},{7,0},{8,9},{9,10},{10,1... | collective-permute-start | bytes 331784 | tf_op jit(solution)/shard_map/ppermute | solution.py:15
  462.3 5.4 copy-start.3
  462.3 5.4 copy-start.12
  467.1 210.9 %all-reduce.4.cloned.1.call-start = ((), (), s32[]{:S(2)}) async-start(), calls=%async_computation.1 | async-start | bytes 3735552 | tf_op jit(solution)/shard_map/psum | solution.py:279
  471.5 7.4 %collective-permute-start = (bf16[8,3,24,192]{3,0,2,1:T(8,128)(2,1)S(1)}, bf16[8,3,24,192]{3,0,2,1:T(8,128)(2,1)S(1)}, u32[]{:S(2)}, u32[]{:S(2)}) collective-permute-start(bf16[8,3,24,192]{3,0,2,1:T(8,128)(2,1)S(1)} %get-tuple-element.403), channel_id=1, source_target_pairs={{0,120},{8,0},{16,8},{24,16},{32,24},{40,32},{48,40},{56,48},{64,5... | collective-permute-start | bytes 663560 | tf_op jit(solution)/shard_map/ppermute | solution.py:15
  478.9 6.1 collective-permute-start.1
  520.2 6.6 copy-start.14
  520.2 6.5 collective-permute-start.2
  522.9 4.8 copy-start.28
  526.7 73.7 %collective-permute-start.3 = (bf16[8,6,6,192]{3,0,2,1:T(8,128)(2,1)S(1)}, bf16[8,6,6,192]{3,0,2,1:T(8,128)(2,1)S(1)}, u32[]{:S(2)}, u32[]{:S(2)}) collective-permute-start(bf16[8,6,6,192]{3,0,2,1:T(8,128)(2,1)S(1)} %pad_maximum_fusion.13), channel_id=1, source_target_pairs={{0,1},{1,2},{2,3},{3,4},{4,5},{5,6},{6,7},{7,0},{8,9},{9,10},{10,1... | collective-permute-start | bytes 331784 | tf_op jit(solution)/shard_map/ppermute | solution.py:15
  (27 other events, 56.8 us)
Sparse Core Ops, SparseCore 0:
  467.2 54.4 all-gather.1
Sparse Core Ops, SparseCore 1:
  523.0 154.9 all-reduce.3
